TPU v7x, 128 devices: a whole 4x4x4 slice. The times are simulated.
128 devices in a mesh: leaf: 4 (over y), dp: 32 (over z, x, core).
Axes of the slice: x: 4, y: 4, z: 4, core: 2. Of those that a mesh axis runs over, the one named last changes fastest.
Arguments:
- bins: int32 [49152, 256], P('dp'), may hold values from 0 to 255
- outcome: float32 [49152], P('dp'), may hold values from -6 to 6
- treatment: int32 [49152], P('dp'), may hold values 0 or 1
- bag: int32 [196608], P(('leaf', 'dp')), parts along dimension 0, may hold values 0 or 1
- block_node: int32 [384], P('dp'), may hold values from 0 to 15, as said below
Outputs:
- hist_sum: float32 [1024, 16, 256], P(('leaf', 'dp')), parts along dimension 0
- hist_count: float32 [1024, 16, 256], P(('leaf', 'dp')), parts along dimension 0
There are 4 independent parts, one for each index of `leaf`. A program takes and returns all parts, laid end to end along the dimension named above; an argument that names none is the same for every part. Nothing has to cross between parts.
Inputs may be any that keep to these rules, and one draw needn't show every extreme that they name: block_node is nondecreasing along the blocks; every node has 1 to 128 blocks, one exactly that many.
All inputs are finite; a program needn't handle non-finite values. No bound on the sum of `treatment` or of `bag` on one device may be relied on, other than what follows from the above.
Results may differ from a plain program's by a relative error of at most 0.0029.
Values may be sent and summed in bfloat16 or wider, within the bound.
No kernel may reach another device: no remote copies, remote signals or barrier semaphores. Data moves between devices by JAX's collectives and lax.ppermute only.
A program may use at most 64 MiB of HBM per device.

v0:
```python
import math
import jax
import jax.numpy as jnp
from jax import lax
from jax.sharding import PartitionSpec as P

BINS = 256
NODES = 16


def node_params(moments):
    count_n = moments[:, 0]
    sum_w = moments[:, 1]
    sum_y = moments[:, 2]
    sum_wy = moments[:, 3]
    shrunk = count_n + 1.0
    wbar = sum_w / shrunk
    ybar = sum_y / shrunk
    cov = sum_wy - wbar * sum_y - ybar * sum_w + count_n * wbar * ybar
    spread = sum_w - 2.0 * wbar * sum_w + count_n * wbar * wbar + 1.0
    effect = cov / spread
    return jnp.stack([wbar, ybar, effect, shrunk / spread], 1)


def histogram_term(bins, left, count):
    row_count = bins.shape[0]
    width = left.shape[1]
    group = math.gcd(count, 16)
    grouped = bins.reshape(row_count, count // group, group).transpose(1, 0, 2)

    def one_group(picked):
        table = (picked[:, :, None] == jnp.arange(BINS, dtype=jnp.int32)[None, None, :]).astype(
            jnp.bfloat16
        )
        return jnp.einsum("rm,rgb->gmb", left, table, preferred_element_type=jnp.float32)

    return lax.map(one_group, grouped).reshape(count, width, BINS)


def shards(bins, outcome, treatment, bag, block_node):
    row_count = bins.shape[0]
    block_count = block_node.shape[0]
    per_block = row_count // block_count
    own_features = bins.shape[1] // lax.axis_size("dp")
    block_hot = (block_node[:, None] == jnp.arange(NODES, dtype=jnp.int32)[None, :]).astype(
        jnp.float32
    )
    weight = treatment.astype(jnp.float32)
    taken = bag.astype(jnp.float32)
    taken_low = taken.astype(jnp.bfloat16)
    stats = jnp.stack([taken, taken * weight, taken * outcome, taken * weight * outcome], 1)
    block_stats = stats.reshape(block_count, per_block, 4).sum(axis=1)
    local_moments = jnp.dot(block_hot.T, block_stats, precision=lax.Precision.HIGHEST)
    row_hot = jnp.repeat(block_hot, per_block, axis=0).astype(jnp.bfloat16)
    count_left = row_hot * taken_low[:, None]
    moments = lax.psum(local_moments, "dp")
    params = node_params(moments)
    block_params = jnp.dot(block_hot, params, precision=lax.Precision.HIGHEST)
    row_params = jnp.repeat(block_params, per_block, axis=0)
    centred = weight - row_params[:, 0]
    rho = (
        taken
        * centred
        * (outcome - row_params[:, 1] - centred * row_params[:, 2])
        * row_params[:, 3]
    )
    rho_low = rho.astype(jnp.bfloat16)
    sum_left = row_hot * rho_low[:, None]
    both_left = jnp.concatenate([sum_left, count_left], axis=1)
    both = lax.psum_scatter(
        histogram_term(bins, both_left, own_features * lax.axis_size("dp")),
        "dp",
        scatter_dimension=0,
        tiled=True,
    )
    hist_sum = both[:, :NODES]
    hist_count = both[:, NODES:]
    return (hist_sum, hist_count)


def solution(mesh):
    return jax.shard_map(
        shards,
        mesh=mesh,
        in_specs=(P("dp", None), P("dp"), P("dp"), P(("leaf", "dp")), P("dp")),
        out_specs=(P(("leaf", "dp"), None, None), P(("leaf", "dp"), None, None)),
        check_vma=False,
    )
```

profile of v0, /device:TPU:0, one launch (start us, length us, event | category | flops | bytes accessed | tf_op | source)
XLA Modules:
  0.0 305.6 jit_solution(4352091207590178504)
XLA Ops:
  7.2 0.0 reduce-scatter.2.cloned.1.call-start
  7.2 0.7 convert_bitcast_fusion
  7.9 0.7 convert_convert_fusion.1
  8.6 0.7 fusion.9
  9.3 0.1 maximum_reduce_fusion
  9.4 0.8 fusion.6
  10.2 68.4 %psum.7 = f32[16,4]{0,1:T(4,128)S(1)} all-reduce(f32[16,4]{0,1:T(4,128)S(1)} %fusion.6), channel_id=1, replica_groups=mesh['leaf'=4,'dp'=32] {'dp'}, use_global_device_ids=true, to_apply=%region_1.0 | all-reduce | flops 64 | bytes 512 | tf_op jit(solution)/shard_map/psum | solution.py:56
  78.6 0.8 fusion.5
  79.4 0.1 broadcast_bitcast_fusion
  79.5 0.1 slice_reduce_fusion.3
  79.6 1.9 copy.11
  81.5 0.7 multiply_convert_fusion
  82.2 0.1 broadcast_in_dim.20
  82.4 125.3 %while.10 = (s32[]{:T(128)}, f32[16,16,32,256]{3,2,1,0:T(8,128)}, s32[16,1536,16]{1,2,0:T(8,128)S(1)}, bf16[1536,32]{0,1:T(8,128)(2,1)S(1)}, s32[]{:T(128)}) while((s32[]{:T(128)}, f32[16,16,32,256]{3,2,1,0:T(8,128)}, s32[16,1536,16]{1,2,0:T(8,128)S(1)}, bf16[1536,32]{0,1:T(8,128)(2,1)S(1)}, s32[]{:T(128)}) %tuple.37), condition=%wide.region_3.4_spmd, body=%wide.region_2.3_spmd.sunk | while | flops 408944640 | bytes 918081 | solution.py:37
  82.4 7.8 %fusion.28 = f32[16,16,32,256]{3,2,1,0:T(8,128)} fusion(f32[16,16,32,256]{3,2,1,0:T(8,128)} %get-tuple-element.80, s32[]{:T(128)} %get-tuple-element.79, s32[1536,16]{0,1:T(8,128)S(1)} %dynamic-slice_bitcast_fusion.2, bf16[1536,32]{0,1:T(8,128)(2,1)S(1)} %get-tuple-element.87), kind=kOutput, calls=%fused_computation.4.clone.1 | convolution fusion | flops 408944640 | bytes 721408 | tf_op jit(solution)/shard_map/while/body/eval_jaxpr/rm,rgb->gmb/dot_general | solution.py:35
  90.2 7.8 %fusion.28 = f32[16,16,32,256]{3,2,1,0:T(8,128)} fusion(f32[16,16,32,256]{3,2,1,0:T(8,128)} %get-tuple-element.80, s32[]{:T(128)} %get-tuple-element.79, s32[1536,16]{0,1:T(8,128)S(1)} %dynamic-slice_bitcast_fusion.2, bf16[1536,32]{0,1:T(8,128)(2,1)S(1)} %get-tuple-element.87), kind=kOutput, calls=%fused_computation.4.clone.1 | convolution fusion | flops 408944640 | bytes 721408 | tf_op jit(solution)/shard_map/while/body/eval_jaxpr/rm,rgb->gmb/dot_general | solution.py:35
  98.1 7.8 %fusion.28 = f32[16,16,32,256]{3,2,1,0:T(8,128)} fusion(f32[16,16,32,256]{3,2,1,0:T(8,128)} %get-tuple-element.80, s32[]{:T(128)} %get-tuple-element.79, s32[1536,16]{0,1:T(8,128)S(1)} %dynamic-slice_bitcast_fusion.2, bf16[1536,32]{0,1:T(8,128)(2,1)S(1)} %get-tuple-element.87), kind=kOutput, calls=%fused_computation.4.clone.1 | convolution fusion | flops 408944640 | bytes 721408 | tf_op jit(solution)/shard_map/while/body/eval_jaxpr/rm,rgb->gmb/dot_general | solution.py:35
  105.9 7.8 %fusion.28 = f32[16,16,32,256]{3,2,1,0:T(8,128)} fusion(f32[16,16,32,256]{3,2,1,0:T(8,128)} %get-tuple-element.80, s32[]{:T(128)} %get-tuple-element.79, s32[1536,16]{0,1:T(8,128)S(1)} %dynamic-slice_bitcast_fusion.2, bf16[1536,32]{0,1:T(8,128)(2,1)S(1)} %get-tuple-element.87), kind=kOutput, calls=%fused_computation.4.clone.1 | convolution fusion | flops 408944640 | bytes 721408 | tf_op jit(solution)/shard_map/while/body/eval_jaxpr/rm,rgb->gmb/dot_general | solution.py:35
  113.7 7.8 %fusion.28 = f32[16,16,32,256]{3,2,1,0:T(8,128)} fusion(f32[16,16,32,256]{3,2,1,0:T(8,128)} %get-tuple-element.80, s32[]{:T(128)} %get-tuple-element.79, s32[1536,16]{0,1:T(8,128)S(1)} %dynamic-slice_bitcast_fusion.2, bf16[1536,32]{0,1:T(8,128)(2,1)S(1)} %get-tuple-element.87), kind=kOutput, calls=%fused_computation.4.clone.1 | convolution fusion | flops 408944640 | bytes 721408 | tf_op jit(solution)/shard_map/while/body/eval_jaxpr/rm,rgb->gmb/dot_general | solution.py:35
  121.6 7.8 %fusion.28 = f32[16,16,32,256]{3,2,1,0:T(8,128)} fusion(f32[16,16,32,256]{3,2,1,0:T(8,128)} %get-tuple-element.80, s32[]{:T(128)} %get-tuple-element.79, s32[1536,16]{0,1:T(8,128)S(1)} %dynamic-slice_bitcast_fusion.2, bf16[1536,32]{0,1:T(8,128)(2,1)S(1)} %get-tuple-element.87), kind=kOutput, calls=%fused_computation.4.clone.1 | convolution fusion | flops 408944640 | bytes 721408 | tf_op jit(solution)/shard_map/while/body/eval_jaxpr/rm,rgb->gmb/dot_general | solution.py:35
  129.4 7.8 %fusion.28 = f32[16,16,32,256]{3,2,1,0:T(8,128)} fusion(f32[16,16,32,256]{3,2,1,0:T(8,128)} %get-tuple-element.80, s32[]{:T(128)} %get-tuple-element.79, s32[1536,16]{0,1:T(8,128)S(1)} %dynamic-slice_bitcast_fusion.2, bf16[1536,32]{0,1:T(8,128)(2,1)S(1)} %get-tuple-element.87), kind=kOutput, calls=%fused_computation.4.clone.1 | convolution fusion | flops 408944640 | bytes 721408 | tf_op jit(solution)/shard_map/while/body/eval_jaxpr/rm,rgb->gmb/dot_general | solution.py:35
  137.2 7.8 %fusion.28 = f32[16,16,32,256]{3,2,1,0:T(8,128)} fusion(f32[16,16,32,256]{3,2,1,0:T(8,128)} %get-tuple-element.80, s32[]{:T(128)} %get-tuple-element.79, s32[1536,16]{0,1:T(8,128)S(1)} %dynamic-slice_bitcast_fusion.2, bf16[1536,32]{0,1:T(8,128)(2,1)S(1)} %get-tuple-element.87), kind=kOutput, calls=%fused_computation.4.clone.1 | convolution fusion | flops 408944640 | bytes 721408 | tf_op jit(solution)/shard_map/while/body/eval_jaxpr/rm,rgb->gmb/dot_general | solution.py:35
  145.1 7.8 %fusion.28 = f32[16,16,32,256]{3,2,1,0:T(8,128)} fusion(f32[16,16,32,256]{3,2,1,0:T(8,128)} %get-tuple-element.80, s32[]{:T(128)} %get-tuple-element.79, s32[1536,16]{0,1:T(8,128)S(1)} %dynamic-slice_bitcast_fusion.2, bf16[1536,32]{0,1:T(8,128)(2,1)S(1)} %get-tuple-element.87), kind=kOutput, calls=%fused_computation.4.clone.1 | convolution fusion | flops 408944640 | bytes 721408 | tf_op jit(solution)/shard_map/while/body/eval_jaxpr/rm,rgb->gmb/dot_general | solution.py:35
  152.9 7.8 %fusion.28 = f32[16,16,32,256]{3,2,1,0:T(8,128)} fusion(f32[16,16,32,256]{3,2,1,0:T(8,128)} %get-tuple-element.80, s32[]{:T(128)} %get-tuple-element.79, s32[1536,16]{0,1:T(8,128)S(1)} %dynamic-slice_bitcast_fusion.2, bf16[1536,32]{0,1:T(8,128)(2,1)S(1)} %get-tuple-element.87), kind=kOutput, calls=%fused_computation.4.clone.1 | convolution fusion | flops 408944640 | bytes 721408 | tf_op jit(solution)/shard_map/while/body/eval_jaxpr/rm,rgb->gmb/dot_general | solution.py:35
  160.7 7.8 %fusion.28 = f32[16,16,32,256]{3,2,1,0:T(8,128)} fusion(f32[16,16,32,256]{3,2,1,0:T(8,128)} %get-tuple-element.80, s32[]{:T(128)} %get-tuple-element.79, s32[1536,16]{0,1:T(8,128)S(1)} %dynamic-slice_bitcast_fusion.2, bf16[1536,32]{0,1:T(8,128)(2,1)S(1)} %get-tuple-element.87), kind=kOutput, calls=%fused_computation.4.clone.1 | convolution fusion | flops 408944640 | bytes 721408 | tf_op jit(solution)/shard_map/while/body/eval_jaxpr/rm,rgb->gmb/dot_general | solution.py:35
  168.5 7.8 %fusion.28 = f32[16,16,32,256]{3,2,1,0:T(8,128)} fusion(f32[16,16,32,256]{3,2,1,0:T(8,128)} %get-tuple-element.80, s32[]{:T(128)} %get-tuple-element.79, s32[1536,16]{0,1:T(8,128)S(1)} %dynamic-slice_bitcast_fusion.2, bf16[1536,32]{0,1:T(8,128)(2,1)S(1)} %get-tuple-element.87), kind=kOutput, calls=%fused_computation.4.clone.1 | convolution fusion | flops 408944640 | bytes 721408 | tf_op jit(solution)/shard_map/while/body/eval_jaxpr/rm,rgb->gmb/dot_general | solution.py:35
  176.4 7.8 %fusion.28 = f32[16,16,32,256]{3,2,1,0:T(8,128)} fusion(f32[16,16,32,256]{3,2,1,0:T(8,128)} %get-tuple-element.80, s32[]{:T(128)} %get-tuple-element.79, s32[1536,16]{0,1:T(8,128)S(1)} %dynamic-slice_bitcast_fusion.2, bf16[1536,32]{0,1:T(8,128)(2,1)S(1)} %get-tuple-element.87), kind=kOutput, calls=%fused_computation.4.clone.1 | convolution fusion | flops 408944640 | bytes 721408 | tf_op jit(solution)/shard_map/while/body/eval_jaxpr/rm,rgb->gmb/dot_general | solution.py:35
  184.2 7.8 %fusion.28 = f32[16,16,32,256]{3,2,1,0:T(8,128)} fusion(f32[16,16,32,256]{3,2,1,0:T(8,128)} %get-tuple-element.80, s32[]{:T(128)} %get-tuple-element.79, s32[1536,16]{0,1:T(8,128)S(1)} %dynamic-slice_bitcast_fusion.2, bf16[1536,32]{0,1:T(8,128)(2,1)S(1)} %get-tuple-element.87), kind=kOutput, calls=%fused_computation.4.clone.1 | convolution fusion | flops 408944640 | bytes 721408 | tf_op jit(solution)/shard_map/while/body/eval_jaxpr/rm,rgb->gmb/dot_general | solution.py:35
  192.0 7.8 %fusion.28 = f32[16,16,32,256]{3,2,1,0:T(8,128)} fusion(f32[16,16,32,256]{3,2,1,0:T(8,128)} %get-tuple-element.80, s32[]{:T(128)} %get-tuple-element.79, s32[1536,16]{0,1:T(8,128)S(1)} %dynamic-slice_bitcast_fusion.2, bf16[1536,32]{0,1:T(8,128)(2,1)S(1)} %get-tuple-element.87), kind=kOutput, calls=%fused_computation.4.clone.1 | convolution fusion | flops 408944640 | bytes 721408 | tf_op jit(solution)/shard_map/while/body/eval_jaxpr/rm,rgb->gmb/dot_general | solution.py:35
  199.9 7.8 %fusion.28 = f32[16,16,32,256]{3,2,1,0:T(8,128)} fusion(f32[16,16,32,256]{3,2,1,0:T(8,128)} %get-tuple-element.80, s32[]{:T(128)} %get-tuple-element.79, s32[1536,16]{0,1:T(8,128)S(1)} %dynamic-slice_bitcast_fusion.2, bf16[1536,32]{0,1:T(8,128)(2,1)S(1)} %get-tuple-element.87), kind=kOutput, calls=%fused_computation.4.clone.1 | convolution fusion | flops 408944640 | bytes 721408 | tf_op jit(solution)/shard_map/while/body/eval_jaxpr/rm,rgb->gmb/dot_general | solution.py:35
  207.7 0.0 reduce-scatter.2.cloned.1.call-update
  207.7 89.4 %reduce-scatter.2.cloned.1.call-done = f32[8,32,256]{2,1,0:T(8,128)} async-done(((f32[256,32,256]{2,1,0:T(8,128)}), f32[8,32,256]{2,1,0:T(8,128)}) %reduce-scatter.2.cloned.1.call-update) | async-done | bytes 262160 | tf_op jit(solution)/shard_map/reduce_scatter | solution.py:70
  297.1 1.7 fusion.23
  (22 shorter events, 0.2 us)
Async XLA Ops:
  7.2 289.9 %reduce-scatter.2.cloned.1.call-start = ((), (), s32[]{:S(2)}) async-start(), calls=%async_computation.1 | async-start | bytes 8650752 | tf_op jit(solution)/shard_map/reduce_scatter | solution.py:70
Sparse Core Ops, SparseCore 0:
  207.8 89.1 reduce-scatter.1
where the time goes:
time: 306 us
  matrix products  127 us (42%)
  waiting for transfers between devices  89.4 us (29%)
  blocking collectives  68.4 us (22%)
  between operations  14.1 us (5%)
  local copies, waits for them, and re-layouts  3.94 us (1%)
    dot_general x16, matrix products, one_group(): jnp.einsum('rm,rgb->gmb', left, table, preferred_element_type=jnp.float32)  125 us
    reduce_scatter x1, waiting for transfers between devices, shards(): lax.psum_scatter(histogram_term(bins, both_left, own_features * lax.axis_...  89.4 us
    psum x1, blocking collectives, shards(): moments = lax.psum(local_moments, 'dp')  68.4 us
  transfers between devices with their start and end apart: 1, of which 1 were waited for; matrix products, arithmetic and copies ran while one was open for 0% of the time, Pallas kernels for 0%

commit v1 on v0

--- a/solution.py
+++ b/solution.py
@@ -53,7 +53,9 @@
     local_moments = jnp.dot(block_hot.T, block_stats, precision=lax.Precision.HIGHEST)
     row_hot = jnp.repeat(block_hot, per_block, axis=0).astype(jnp.bfloat16)
     count_left = row_hot * taken_low[:, None]
-    moments = lax.psum(local_moments, "dp")
+    moments = local_moments
+    for hop in (1, 2, 4, 8, 16):
+        moments = moments + lax.ppermute(moments, "dp", [(dev, dev ^ hop) for dev in range(32)])
     params = node_params(moments)
     block_params = jnp.dot(block_hot, params, precision=lax.Precision.HIGHEST)
     row_params = jnp.repeat(block_params, per_block, axis=0)

time: 306 us -> 260 us (0.85)
  blocking collectives: 68.4 us -> 0 us
  waiting for transfers between devices: 89.4 us -> 101 us
  starting transfers between devices: 0.04 us -> 10.7 us
    psum x1 -> x0, blocking collectives: 68.4 us -> none  [shards(): moments = lax.psum(local_moments, 'dp')]
    ppermute x0 -> x5, starting transfers between devices: none -> 10.6 us  [shards(): lax.ppermute(moments, 'dp', [(dev, dev ^ hop) for dev in range(32)])]
    ppermute x0 -> x5, waiting for transfers between devices: none -> 6.07 us  [shards(): lax.ppermute(moments, 'dp', [(dev, dev ^ hop) for dev in range(32)])]
    reduce_scatter x1, waiting for transfers between devices: 89.4 us -> 94.6 us  [shards(): lax.psum_scatter(histogram_term(bins, both_left, own_features * lax.axis_...]
  transfers between devices with their start and end apart: 1 -> 6, of which waited for: 1 -> 5; matrix products, arithmetic and copies ran while one was open for 0% -> 1% of each run, Pallas kernels for 0% -> 0%
where the time goes in v1:
time: 260 us; the launch traced here: 259 us
  matrix products  127 us (49%)
  waiting for transfers between devices  101 us (39%)
  between operations  14.1 us (5%)
  starting transfers between devices  10.7 us (4%)
  local copies, waits for them, and re-layouts  3.94 us (2%)
  other arithmetic  3 us (1%)
    dot_general x16, matrix products, one_group(): jnp.einsum('rm,rgb->gmb', left, table, preferred_element_type=jnp.float32)  125 us
    reduce_scatter x1, waiting for transfers between devices, shards(): lax.psum_scatter(histogram_term(bins, both_left, own_features * lax.axis_...  94.6 us
    ppermute x5, starting transfers between devices, shards(): lax.ppermute(moments, 'dp', [(dev, dev ^ hop) for dev in range(32)])  10.6 us
    ppermute x5, waiting for transfers between devices, shards(): lax.ppermute(moments, 'dp', [(dev, dev ^ hop) for dev in range(32)])  6.07 us
  transfers between devices with their start and end apart: 6, of which 5 were waited for; matrix products, arithmetic and copies ran while one was open for 1% of the time, Pallas kernels for 0%

profile of v1, /device:TPU:0, one launch (start us, length us, event | category | flops | bytes accessed | tf_op | source)
XLA Modules:
  0.0 259.2 jit_solution(12511162113011069848)
XLA Ops:
  7.2 0.0 reduce-scatter.2.cloned.1.call-start
  7.2 0.7 convert_bitcast_fusion
  7.9 0.7 fusion.9
  8.6 0.1 maximum_reduce_fusion
  8.7 0.8 fusion.6
  9.5 0.0 collective-permute-start
  9.5 1.2 collective-permute-done
  10.7 1.6 collective-permute-start.1
  12.2 2.0 collective-permute-done.1
  14.3 3.1 %collective-permute-start.2 = (f32[16,4]{0,1:T(4,128)S(1)}, f32[16,4]{0,1:T(4,128)S(1)}, u32[]{:S(2)}, u32[]{:S(2)}) collective-permute-start(f32[16,4]{0,1:T(4,128)S(1)} %add.42), channel_id=1, source_target_pairs={{0,4},{1,5},{2,6},{3,7},{4,0},{5,1},{6,2},{7,3},{8,12},{9,13},{10,... | collective-permute-start | bytes 776 | tf_op jit(solution)/shard_map/ppermute | solution.py:58
  17.4 2.0 collective-permute-done.2
  19.4 2.0 collective-permute-start.3
  21.4 0.7 convert_convert_fusion.1
  22.0 0.9 collective-permute-done.3
  22.9 4.0 %collective-permute-start.4 = (f32[16,4]{0,1:T(4,128)S(1)}, f32[16,4]{0,1:T(4,128)S(1)}, u32[]{:S(2)}, u32[]{:S(2)}) collective-permute-start(f32[16,4]{0,1:T(4,128)S(1)} %add.44), channel_id=1, source_target_pairs={{0,16},{1,17},{2,18},{3,19},{4,20},{5,21},{6,22},{7,23},{8,24},{9,... | collective-permute-start | bytes 776 | tf_op jit(solution)/shard_map/ppermute | solution.py:58
  26.9 1.9 copy.11
  28.8 0.0 collective-permute-done.4
  28.8 0.8 fusion.5
  29.6 0.1 broadcast_bitcast_fusion
  29.7 0.1 slice_reduce_fusion.3
  29.8 0.7 multiply_convert_fusion
  30.5 0.1 broadcast_in_dim.20
  30.7 125.3 %while.10 = (s32[]{:T(128)}, f32[16,16,32,256]{3,2,1,0:T(8,128)}, s32[16,1536,16]{1,2,0:T(8,128)S(1)}, bf16[1536,32]{0,1:T(8,128)(2,1)S(1)}, s32[]{:T(128)}) while((s32[]{:T(128)}, f32[16,16,32,256]{3,2,1,0:T(8,128)}, s32[16,1536,16]{1,2,0:T(8,128)S(1)}, bf16[1536,32]{0,1:T(8,128)(2,1)S(1)}, s32[]{:T(128)}) %tuple.37), condition=%wide.region_2.3_spmd, body=%wide.region_1.2_spmd.sunk | while | flops 408944640 | bytes 918081 | solution.py:37
  30.7 7.8 %fusion.28 = f32[16,16,32,256]{3,2,1,0:T(8,128)} fusion(f32[16,16,32,256]{3,2,1,0:T(8,128)} %get-tuple-element.80, s32[]{:T(128)} %get-tuple-element.79, s32[1536,16]{0,1:T(8,128)S(1)} %dynamic-slice_bitcast_fusion.2, bf16[1536,32]{0,1:T(8,128)(2,1)S(1)} %get-tuple-element.87), kind=kOutput, calls=%fused_computation.4.clone.1 | convolution fusion | flops 408944640 | bytes 721408 | tf_op jit(solution)/shard_map/while/body/eval_jaxpr/rm,rgb->gmb/dot_general | solution.py:35
  38.6 7.8 %fusion.28 = f32[16,16,32,256]{3,2,1,0:T(8,128)} fusion(f32[16,16,32,256]{3,2,1,0:T(8,128)} %get-tuple-element.80, s32[]{:T(128)} %get-tuple-element.79, s32[1536,16]{0,1:T(8,128)S(1)} %dynamic-slice_bitcast_fusion.2, bf16[1536,32]{0,1:T(8,128)(2,1)S(1)} %get-tuple-element.87), kind=kOutput, calls=%fused_computation.4.clone.1 | convolution fusion | flops 408944640 | bytes 721408 | tf_op jit(solution)/shard_map/while/body/eval_jaxpr/rm,rgb->gmb/dot_general | solution.py:35
  46.4 7.8 %fusion.28 = f32[16,16,32,256]{3,2,1,0:T(8,128)} fusion(f32[16,16,32,256]{3,2,1,0:T(8,128)} %get-tuple-element.80, s32[]{:T(128)} %get-tuple-element.79, s32[1536,16]{0,1:T(8,128)S(1)} %dynamic-slice_bitcast_fusion.2, bf16[1536,32]{0,1:T(8,128)(2,1)S(1)} %get-tuple-element.87), kind=kOutput, calls=%fused_computation.4.clone.1 | convolution fusion | flops 408944640 | bytes 721408 | tf_op jit(solution)/shard_map/while/body/eval_jaxpr/rm,rgb->gmb/dot_general | solution.py:35
  54.2 7.8 %fusion.28 = f32[16,16,32,256]{3,2,1,0:T(8,128)} fusion(f32[16,16,32,256]{3,2,1,0:T(8,128)} %get-tuple-element.80, s32[]{:T(128)} %get-tuple-element.79, s32[1536,16]{0,1:T(8,128)S(1)} %dynamic-slice_bitcast_fusion.2, bf16[1536,32]{0,1:T(8,128)(2,1)S(1)} %get-tuple-element.87), kind=kOutput, calls=%fused_computation.4.clone.1 | convolution fusion | flops 408944640 | bytes 721408 | tf_op jit(solution)/shard_map/while/body/eval_jaxpr/rm,rgb->gmb/dot_general | solution.py:35
  62.1 7.8 %fusion.28 = f32[16,16,32,256]{3,2,1,0:T(8,128)} fusion(f32[16,16,32,256]{3,2,1,0:T(8,128)} %get-tuple-element.80, s32[]{:T(128)} %get-tuple-element.79, s32[1536,16]{0,1:T(8,128)S(1)} %dynamic-slice_bitcast_fusion.2, bf16[1536,32]{0,1:T(8,128)(2,1)S(1)} %get-tuple-element.87), kind=kOutput, calls=%fused_computation.4.clone.1 | convolution fusion | flops 408944640 | bytes 721408 | tf_op jit(solution)/shard_map/while/body/eval_jaxpr/rm,rgb->gmb/dot_general | solution.py:35
  69.9 7.8 %fusion.28 = f32[16,16,32,256]{3,2,1,0:T(8,128)} fusion(f32[16,16,32,256]{3,2,1,0:T(8,128)} %get-tuple-element.80, s32[]{:T(128)} %get-tuple-element.79, s32[1536,16]{0,1:T(8,128)S(1)} %dynamic-slice_bitcast_fusion.2, bf16[1536,32]{0,1:T(8,128)(2,1)S(1)} %get-tuple-element.87), kind=kOutput, calls=%fused_computation.4.clone.1 | convolution fusion | flops 408944640 | bytes 721408 | tf_op jit(solution)/shard_map/while/body/eval_jaxpr/rm,rgb->gmb/dot_general | solution.py:35
  77.7 7.8 %fusion.28 = f32[16,16,32,256]{3,2,1,0:T(8,128)} fusion(f32[16,16,32,256]{3,2,1,0:T(8,128)} %get-tuple-element.80, s32[]{:T(128)} %get-tuple-element.79, s32[1536,16]{0,1:T(8,128)S(1)} %dynamic-slice_bitcast_fusion.2, bf16[1536,32]{0,1:T(8,128)(2,1)S(1)} %get-tuple-element.87), kind=kOutput, calls=%fused_computation.4.clone.1 | convolution fusion | flops 408944640 | bytes 721408 | tf_op jit(solution)/shard_map/while/body/eval_jaxpr/rm,rgb->gmb/dot_general | solution.py:35
  85.6 7.8 %fusion.28 = f32[16,16,32,256]{3,2,1,0:T(8,128)} fusion(f32[16,16,32,256]{3,2,1,0:T(8,128)} %get-tuple-element.80, s32[]{:T(128)} %get-tuple-element.79, s32[1536,16]{0,1:T(8,128)S(1)} %dynamic-slice_bitcast_fusion.2, bf16[1536,32]{0,1:T(8,128)(2,1)S(1)} %get-tuple-element.87), kind=kOutput, calls=%fused_computation.4.clone.1 | convolution fusion | flops 408944640 | bytes 721408 | tf_op jit(solution)/shard_map/while/body/eval_jaxpr/rm,rgb->gmb/dot_general | solution.py:35
  93.4 7.8 %fusion.28 = f32[16,16,32,256]{3,2,1,0:T(8,128)} fusion(f32[16,16,32,256]{3,2,1,0:T(8,128)} %get-tuple-element.80, s32[]{:T(128)} %get-tuple-element.79, s32[1536,16]{0,1:T(8,128)S(1)} %dynamic-slice_bitcast_fusion.2, bf16[1536,32]{0,1:T(8,128)(2,1)S(1)} %get-tuple-element.87), kind=kOutput, calls=%fused_computation.4.clone.1 | convolution fusion | flops 408944640 | bytes 721408 | tf_op jit(solution)/shard_map/while/body/eval_jaxpr/rm,rgb->gmb/dot_general | solution.py:35
  101.2 7.8 %fusion.28 = f32[16,16,32,256]{3,2,1,0:T(8,128)} fusion(f32[16,16,32,256]{3,2,1,0:T(8,128)} %get-tuple-element.80, s32[]{:T(128)} %get-tuple-element.79, s32[1536,16]{0,1:T(8,128)S(1)} %dynamic-slice_bitcast_fusion.2, bf16[1536,32]{0,1:T(8,128)(2,1)S(1)} %get-tuple-element.87), kind=kOutput, calls=%fused_computation.4.clone.1 | convolution fusion | flops 408944640 | bytes 721408 | tf_op jit(solution)/shard_map/while/body/eval_jaxpr/rm,rgb->gmb/dot_general | solution.py:35
  109.0 7.8 %fusion.28 = f32[16,16,32,256]{3,2,1,0:T(8,128)} fusion(f32[16,16,32,256]{3,2,1,0:T(8,128)} %get-tuple-element.80, s32[]{:T(128)} %get-tuple-element.79, s32[1536,16]{0,1:T(8,128)S(1)} %dynamic-slice_bitcast_fusion.2, bf16[1536,32]{0,1:T(8,128)(2,1)S(1)} %get-tuple-element.87), kind=kOutput, calls=%fused_computation.4.clone.1 | convolution fusion | flops 408944640 | bytes 721408 | tf_op jit(solution)/shard_map/while/body/eval_jaxpr/rm,rgb->gmb/dot_general | solution.py:35
  116.9 7.8 %fusion.28 = f32[16,16,32,256]{3,2,1,0:T(8,128)} fusion(f32[16,16,32,256]{3,2,1,0:T(8,128)} %get-tuple-element.80, s32[]{:T(128)} %get-tuple-element.79, s32[1536,16]{0,1:T(8,128)S(1)} %dynamic-slice_bitcast_fusion.2, bf16[1536,32]{0,1:T(8,128)(2,1)S(1)} %get-tuple-element.87), kind=kOutput, calls=%fused_computation.4.clone.1 | convolution fusion | flops 408944640 | bytes 721408 | tf_op jit(solution)/shard_map/while/body/eval_jaxpr/rm,rgb->gmb/dot_general | solution.py:35
  124.7 7.8 %fusion.28 = f32[16,16,32,256]{3,2,1,0:T(8,128)} fusion(f32[16,16,32,256]{3,2,1,0:T(8,128)} %get-tuple-element.80, s32[]{:T(128)} %get-tuple-element.79, s32[1536,16]{0,1:T(8,128)S(1)} %dynamic-slice_bitcast_fusion.2, bf16[1536,32]{0,1:T(8,128)(2,1)S(1)} %get-tuple-element.87), kind=kOutput, calls=%fused_computation.4.clone.1 | convolution fusion | flops 408944640 | bytes 721408 | tf_op jit(solution)/shard_map/while/body/eval_jaxpr/rm,rgb->gmb/dot_general | solution.py:35
  132.5 7.8 %fusion.28 = f32[16,16,32,256]{3,2,1,0:T(8,128)} fusion(f32[16,16,32,256]{3,2,1,0:T(8,128)} %get-tuple-element.80, s32[]{:T(128)} %get-tuple-element.79, s32[1536,16]{0,1:T(8,128)S(1)} %dynamic-slice_bitcast_fusion.2, bf16[1536,32]{0,1:T(8,128)(2,1)S(1)} %get-tuple-element.87), kind=kOutput, calls=%fused_computation.4.clone.1 | convolution fusion | flops 408944640 | bytes 721408 | tf_op jit(solution)/shard_map/while/body/eval_jaxpr/rm,rgb->gmb/dot_general | solution.py:35
  140.4 7.8 %fusion.28 = f32[16,16,32,256]{3,2,1,0:T(8,128)} fusion(f32[16,16,32,256]{3,2,1,0:T(8,128)} %get-tuple-element.80, s32[]{:T(128)} %get-tuple-element.79, s32[1536,16]{0,1:T(8,128)S(1)} %dynamic-slice_bitcast_fusion.2, bf16[1536,32]{0,1:T(8,128)(2,1)S(1)} %get-tuple-element.87), kind=kOutput, calls=%fused_computation.4.clone.1 | convolution fusion | flops 408944640 | bytes 721408 | tf_op jit(solution)/shard_map/while/body/eval_jaxpr/rm,rgb->gmb/dot_general | solution.py:35
  148.2 7.8 %fusion.28 = f32[16,16,32,256]{3,2,1,0:T(8,128)} fusion(f32[16,16,32,256]{3,2,1,0:T(8,128)} %get-tuple-element.80, s32[]{:T(128)} %get-tuple-element.79, s32[1536,16]{0,1:T(8,128)S(1)} %dynamic-slice_bitcast_fusion.2, bf16[1536,32]{0,1:T(8,128)(2,1)S(1)} %get-tuple-element.87), kind=kOutput, calls=%fused_computation.4.clone.1 | convolution fusion | flops 408944640 | bytes 721408 | tf_op jit(solution)/shard_map/while/body/eval_jaxpr/rm,rgb->gmb/dot_general | solution.py:35
  156.0 0.0 reduce-scatter.2.cloned.1.call-update
  156.1 94.6 %reduce-scatter.2.cloned.1.call-done = f32[8,32,256]{2,1,0:T(8,128)} async-done(((f32[256,32,256]{2,1,0:T(8,128)}), f32[8,32,256]{2,1,0:T(8,128)}) %reduce-scatter.2.cloned.1.call-update) | async-done | bytes 262160 | tf_op jit(solution)/shard_map/reduce_scatter | solution.py:72
  250.7 1.7 fusion.23
  (27 shorter events, 0.2 us)
Async XLA Ops:
  7.2 243.5 %reduce-scatter.2.cloned.1.call-start = ((), (), s32[]{:S(2)}) async-start(), calls=%async_computation.1 | async-start | bytes 8650752 | tf_op jit(solution)/shard_map/reduce_scatter | solution.py:72
  9.5 1.2 collective-permute-start
  10.7 3.6 %collective-permute-start.1 = (f32[16,4]{0,1:T(4,128)S(1)}, f32[16,4]{0,1:T(4,128)S(1)}, u32[]{:S(2)}, u32[]{:S(2)}) collective-permute-start(f32[16,4]{0,1:T(4,128)S(1)} %add.41), channel_id=1, source_target_pairs={{0,2},{1,3},{2,0},{3,1},{4,6},{5,7},{6,4},{7,5},{8,10},{9,11},{10,... | collective-permute-start | bytes 776 | tf_op jit(solution)/shard_map/ppermute | solution.py:58
  14.3 5.1 %collective-permute-start.2 = (f32[16,4]{0,1:T(4,128)S(1)}, f32[16,4]{0,1:T(4,128)S(1)}, u32[]{:S(2)}, u32[]{:S(2)}) collective-permute-start(f32[16,4]{0,1:T(4,128)S(1)} %add.42), channel_id=1, source_target_pairs={{0,4},{1,5},{2,6},{3,7},{4,0},{5,1},{6,2},{7,3},{8,12},{9,13},{10,... | collective-permute-start | bytes 776 | tf_op jit(solution)/shard_map/ppermute | solution.py:58
  19.4 3.6 %collective-permute-start.3 = (f32[16,4]{0,1:T(4,128)S(1)}, f32[16,4]{0,1:T(4,128)S(1)}, u32[]{:S(2)}, u32[]{:S(2)}) collective-permute-start(f32[16,4]{0,1:T(4,128)S(1)} %add.43), channel_id=1, source_target_pairs={{0,8},{1,9},{2,10},{3,11},{4,12},{5,13},{6,14},{7,15},{8,0},{9,1},... | collective-permute-start | bytes 776 | tf_op jit(solution)/shard_map/ppermute | solution.py:58
  22.9 5.8 %collective-permute-start.4 = (f32[16,4]{0,1:T(4,128)S(1)}, f32[16,4]{0,1:T(4,128)S(1)}, u32[]{:S(2)}, u32[]{:S(2)}) collective-permute-start(f32[16,4]{0,1:T(4,128)S(1)} %add.44), channel_id=1, source_target_pairs={{0,16},{1,17},{2,18},{3,19},{4,20},{5,21},{6,22},{7,23},{8,24},{9,... | collective-permute-start | bytes 776 | tf_op jit(solution)/shard_map/ppermute | solution.py:58
Sparse Core Ops, SparseCore 0:
  156.2 94.4 reduce-scatter.1
